TPU v7x, 32 devices: a whole 2x2x4 slice. The times are simulated.
32 devices in a mesh: lib: 2 (over x), hit: 8 (over z, y), lm: 2 (over core).
Axes of the slice: x: 2, y: 2, z: 4, core: 2. Of those that a mesh axis runs over, the one named last changes fastest.
Arguments:
- fingerprints: int32 [8192, 128], P(('lib', 'hit')), parts along dimension 0, may hold values from 0 to 65535, as said below
- pick_list: int32 [8192], P(('lib', 'lm')), parts along dimension 0, may hold values from 0 to 4095, as said below
- inverse_root: bfloat16 [8192, 2, 2048], P('lib', 'lm', 'hit'), parts along dimension 0, may hold values from -0.09375 to 0.09375
Outputs:
- embedding: bfloat16 [8192, 4096], P(('lib', 'hit'), 'lm'), parts along dimension 0
There are 2 independent parts, one for each index of `lib`. A program takes and returns all parts, laid end to end along the dimension named above; each array names one. Nothing has to cross between parts.
Inputs may be any that keep to these rules, and one draw needn't show every extreme that they name: `pick_list`: within each half of the list, at most 768 picks lie in any one aligned block of 512 hits, and exactly 768 lie in one such block. `fingerprints`: every fingerprint has the lowest bit of its first word set.
All inputs are finite; a program needn't handle non-finite values.
Results may differ from a plain program's by a relative error of at most 0.0049.
Values may be sent and summed in bfloat16 or wider, within the bound.
No kernel may reach another device: no remote copies, remote signals or barrier semaphores. Data moves between devices by JAX's collectives and lax.ppermute only.
A program may use at most 128 MiB of HBM per device.

v0:
```python
import jax
import jax.numpy as jnp
from jax import lax
from jax.sharding import PartitionSpec as P


def unpack_words(packed):
    shifts = jnp.arange(16, dtype=jnp.int32)
    flags = jnp.bitwise_and(jnp.right_shift(packed[:, :, None], shifts[None, None, :]), 1)
    return flags.reshape(packed.shape[0], packed.shape[1] * 16).astype(jnp.bfloat16)


def local(fingerprints, pick_list, inverse_root):
    hit_rows = fingerprints.shape[0]
    hit_devices = lax.axis_size("hit")
    my_index = lax.axis_index("hit")
    holder = pick_list // hit_rows
    row_local = pick_list - holder * hit_rows
    is_mine = holder == my_index
    safe_row = jnp.where(is_mine, row_local, 0)
    picked = jnp.where(is_mine[:, None], fingerprints[safe_row], 0)
    landmark_words = lax.pmax(picked, "hit")
    hit_bits = unpack_words(fingerprints)
    landmark_bits = unpack_words(landmark_words)
    common = lax.dot_general(
        hit_bits, landmark_bits, (((1,), (1,)), ((), ())), preferred_element_type=jnp.float32
    )
    hit_count = jnp.sum(hit_bits, axis=1, dtype=jnp.float32)
    landmark_count = jnp.sum(landmark_bits, axis=1, dtype=jnp.float32)
    kernel = (common / (hit_count[:, None] + landmark_count[None, :] - common)).astype(jnp.bfloat16)
    weight = inverse_root[:, 0, :]
    block_cols = weight.shape[1]
    halves = lax.all_to_all(weight, "lm", split_axis=0, concat_axis=1, tiled=True)
    partial_sum = jnp.dot(
        kernel,
        lax.all_gather(halves, "hit", axis=1, tiled=True),
        preferred_element_type=jnp.float32,
    )
    partial_sum = partial_sum.reshape(hit_rows, hit_devices, 2, block_cols)
    partial_sum = partial_sum.transpose(0, 2, 1, 3).reshape(hit_rows, 2 * hit_devices * block_cols)
    embedding = lax.psum_scatter(partial_sum, "lm", scatter_dimension=1, tiled=True)
    return embedding.astype(jnp.bfloat16)


def solution(mesh):
    placed = (P(("lib", "hit"), None), P(("lib", "lm")), P("lib", "lm", "hit"))
    return jax.shard_map(
        local, mesh=mesh, in_specs=placed, out_specs=P(("lib", "hit"), "lm"), check_vma=False
    )
```

profile of v0, /device:TPU:0, one launch (start us, length us, event | category | flops | bytes accessed | tf_op | source)
XLA Modules:
  0.0 393.9 jit_solution(12185219296085052404)
XLA Ops:
  6.5 0.0 all-reduce.2.cloned.1.call-start
  6.5 0.7 fusion.9
  7.2 0.7 fusion.7
  8.0 6.4 %gather_fusion = s32[2048,128]{1,0:T(8,128)S(1)} fusion(s32[512,128]{1,0:T(8,128)} %param.3, s32[2048]{0:T(1024)S(1)} %fusion.7), kind=kCustom, calls=%fused_computation | custom fusion | bytes 2105344 | tf_op jit(solution)/shard_map/gather | solution.py:21
  14.4 1.4 broadcast_select_fusion
  15.7 0.0 all-reduce.2.cloned.1.call-update
  15.8 0.0 all-gather.2.cloned.1.call-start
  15.8 6.6 %all_to_all.19 = bf16[2,2048,256]{2,1,0:T(8,128)(2,1)S(1)} all-to-all(bf16[2,2048,256]{2,1,0:T(8,128)(2,1)} %bitcast.28), channel_id=1, replica_groups=mesh['lib'=2,'hit'=8,'lm'=2] {'lm'}, dimensions={0} | all-to-all | bytes 4194304 | tf_op jit(solution)/shard_map/all_to_all | solution.py:33
  22.4 0.0 copy-start
  22.4 2.4 copy.6
  24.8 0.0 all-gather.2.cloned.1.call-update
  24.8 0.0 reduce-scatter.2.cloned.1.call-start
  24.9 0.0 copy-done
  24.9 0.6 convert_reduce_fusion.1
  25.5 71.4 %all-reduce.2.cloned.1.call-done = s32[2048,128]{1,0:T(8,128)} async-done(((s32[2048,128]{1,0:T(8,128)}), s32[2048,128]{1,0:T(8,128)}) %all-reduce.2.cloned.1.call-update) | async-done | bytes 1048592 | tf_op jit(solution)/shard_map/pmax | solution.py:22
  96.9 3.4 convert_reduce_fusion
  100.3 6.0 %fusion.17 = bf16[512,2048]{1,0:T(8,128)(2,1)S(1)} fusion(f32[2048]{0:T(1024)S(1)} %convert_reduce_fusion, f32[512]{0:T(512)S(1)} %convert_reduce_fusion.1, s32[2048,128]{1,0:T(8,128)} %all-reduce.2.cloned.1.call-done, s32[512,128]{1,0:T(8,128)S(1)} %copy-done), kind=kOutput, calls=%bitcast_fusion.clone.1 | convolution fusion | flops 4314890240 | bytes 3418112 | tf_op jit(solution)/shard_map/dot_general | solution.py:25
  106.3 220.0 %all-gather.2.cloned.1.call-done = bf16[2048,4096]{0,1:T(8,128)(2,1)} async-done(((bf16[2048,512]{0,1:T(8,128)(2,1)}), bf16[2048,4096]{0,1:T(8,128)(2,1)}) %all-gather.2.cloned.1.call-update) | async-done | bytes 16777232 | tf_op jit(solution)/shard_map/all_gather | solution.py:36
  326.3 14.7 %fusion.11 = f32[512,4096]{1,0:T(8,128)} fusion(bf16[2048,4096]{0,1:T(8,128)(2,1)} %all-gather.2.cloned.1.call-done, bf16[512,2048]{1,0:T(8,128)(2,1)S(1)} %fusion.17), kind=kOutput, calls=%fused_computation.24 | convolution fusion | flops 8589934592 | bytes 27262976 | tf_op jit(solution)/shard_map/dot_general | solution.py:34
  340.9 11.7 %reshape.43 = f32[512,8,2,256]{3,2,1,0:T(2,128)} reshape(f32[512,4096]{1,0:T(8,128)} %fusion.11) | data formatting | bytes 16777216 | tf_op jit(solution)/shard_map/reshape | solution.py:39
  352.7 4.4 %copy.7 = f32[512,2,8,256]{3,2,1,0:T(8,128)S(1)} copy(f32[512,2,8,256]{3,1,2,0:T(2,128)} %bitcast.24) | data formatting | bytes 16777216 | tf_op jit(solution)/shard_map/transpose | solution.py:40
  357.0 11.3 %copy.8 = f32[64,8,16,256]{3,1,2,0:T(8,128)} copy(f32[64,8,16,256]{3,2,1,0:T(8,128)S(1)} %bitcast.25) | data formatting | bytes 16777216
  368.4 0.0 reduce-scatter.2.cloned.1.call-update
  368.4 15.1 %reduce-scatter.2.cloned.1.call-done = f32[512,2048]{1,0:T(8,128)} async-done(((f32[512,4096]{1,0:T(8,128)}), f32[512,2048]{1,0:T(8,128)}) %reduce-scatter.2.cloned.1.call-update) | async-done | bytes 4194320 | tf_op jit(solution)/shard_map/reduce_scatter | solution.py:41
  383.5 3.8 convert_element_type.29
Async XLA Ops:
  6.5 90.3 %all-reduce.2.cloned.1.call-start = ((), (), s32[]{:S(2)}) async-start(), calls=%async_computation.2 | async-start | bytes 2097152 | tf_op jit(solution)/shard_map/pmax | solution.py:22
  15.8 310.5 %all-gather.2.cloned.1.call-start = ((), (), s32[]{:S(2)}) async-start(), calls=%async_computation.3 | async-start | bytes 18874368 | tf_op jit(solution)/shard_map/all_gather | solution.py:36
  22.4 2.4 copy-start
  24.8 358.7 %reduce-scatter.2.cloned.1.call-start = ((), (), s32[]{:S(2)}) async-start(), calls=%async_computation.4 | async-start | bytes 12582912 | tf_op jit(solution)/shard_map/reduce_scatter | solution.py:41
Sparse Core Ops, SparseCore 0:
  15.9 80.9 all-reduce.1
  99.0 227.1 all-gather.1
  368.5 14.9 reduce-scatter.1
where the time goes:
time: 395 us; the launch traced here: 394 us
  waiting for transfers between devices  307 us (78%)
  local copies, waits for them, and re-layouts  36.2 us (9%)
  matrix products  20.7 us (5%)
  between operations  13.1 us (3%)
  other arithmetic  10.7 us (3%)
  blocking collectives  6.63 us (2%)
    all_gather x1, waiting for transfers between devices, local(): lax.all_gather(halves, 'hit', axis=1, tiled=True)  220 us
    pmax x1, waiting for transfers between devices, local(): landmark_words = lax.pmax(picked, 'hit')  71.4 us
    reduce_scatter x1, waiting for transfers between devices, local(): lax.psum_scatter(partial_sum, 'lm', scatter_dimension=1, tiled=True)  15.1 us
    dot_general x1, matrix products, local(): jnp.dot(kernel, lax.all_gather(halves, 'hit', axis=1, tiled=True), prefer...  14.7 us
    reshape x1, local copies, waits for them, and re-layouts, local(): partial_sum = partial_sum.reshape(hit_rows, hit_devices, 2, block_cols)  11.7 us
    unnamed x3, local copies, waits for them, and re-layouts  11.3 us
  transfers between devices with their start and end apart: 3, of which 3 were waited for; matrix products, arithmetic and copies ran while one was open for 3% of the time, Pallas kernels for 0%

commit v1 on v0

v1 whole, which is shorter than its diff:
```python
import functools

import jax
import jax.numpy as jnp
from jax import lax
from jax.experimental import pallas as pl
from jax.experimental.pallas import tpu as pltpu
from jax.sharding import PartitionSpec as P

F8 = jnp.float8_e4m3fn
BITS = 16
VMEM = pl.BlockSpec(memory_space=pltpu.VMEM)
SMEM = pl.BlockSpec(memory_space=pltpu.SMEM)


def unpack_kernel(*refs):
    half = len(refs) // 3
    for word_ref, bits_ref, count_ref in zip(refs[:half], refs[half::2], refs[half + 1 :: 2]):
        words = word_ref[...].astype(jnp.int32)
        count = jnp.sum(lax.population_count(words).astype(jnp.float32), axis=1, keepdims=True)
        count_ref[...] = jnp.broadcast_to(count, count_ref.shape)
        width = words.shape[1]
        for bit in range(BITS):
            flag = ((words >> bit) & 1).astype(jnp.int8)
            bits_ref[:, bit * width : (bit + 1) * width] = flag.astype(F8)


def unpack(blocks):
    shapes = []
    for block in blocks:
        rows, width = block.shape
        shapes.append(jax.ShapeDtypeStruct((rows, BITS * width), F8))
        shapes.append(jax.ShapeDtypeStruct((rows, 128), jnp.float32))
    out = pl.pallas_call(
        unpack_kernel,
        in_specs=[VMEM] * len(blocks),
        out_specs=[VMEM] * len(shapes),
        out_shape=shapes,
        compiler_params=pltpu.CompilerParams(vmem_limit_bytes=24 * 2**20),
        name="unpack",
    )(*blocks)
    return [(out[2 * i], out[2 * i + 1]) for i in range(len(blocks))]


def spread_kernel(base_ref, pick_ref, weight_ref, out_ref, *, sub, chunk):
    step = pl.program_id(0)
    tile = out_ref.shape[1]
    parts = [
        lax.broadcasted_iota(jnp.int32, (sub, 1), 0) + base_ref[step * (tile // sub) + i]
        for i in range(tile // sub)
    ]
    ids = jnp.concatenate(parts, axis=0)
    total = None
    for start in range(0, weight_ref.shape[0], chunk):
        hot = jnp.where(pick_ref[0:1, start : start + chunk] == ids, 1.0, 0.0).astype(jnp.bfloat16)
        part = jnp.dot(
            hot, weight_ref[start : start + chunk, :], preferred_element_type=jnp.float32
        )
        total = part if total is None else total + part
    out_ref[...] = total.T.astype(jnp.bfloat16)


def spread(base, picks, weight, sub, tile=1024, chunk=512):
    marks, cols = weight.shape
    hits = base.shape[0] * sub
    return pl.pallas_call(
        functools.partial(spread_kernel, sub=sub, chunk=chunk),
        grid_spec=pltpu.PrefetchScalarGridSpec(
            num_scalar_prefetch=1,
            grid=(hits // tile,),
            in_specs=[
                pl.BlockSpec((1, marks), lambda i, base: (0, 0)),
                pl.BlockSpec((marks, cols), lambda i, base: (0, 0)),
            ],
            out_specs=pl.BlockSpec((cols, tile), lambda i, base: (0, i)),
        ),
        out_shape=jax.ShapeDtypeStruct((cols, hits), jnp.bfloat16),
        compiler_params=pltpu.CompilerParams(vmem_limit_bytes=24 * 2**20),
        cost_estimate=pl.CostEstimate(
            flops=2 * marks * cols * hits, bytes_accessed=4 * marks * cols, transcendentals=0
        ),
        name="spread",
    )(base, picks, weight)


def block_kernel(words_ref, own_ref, sib_ref, *refs):
    out_ref, flags, kern = refs[-3:]
    pairs = refs[:-3]
    words = words_ref[...].astype(jnp.int32).T
    width = words.shape[0]
    count = jnp.sum(lax.population_count(words).astype(jnp.float32), axis=0, keepdims=True)
    for bit in range(BITS):
        flag = ((words >> bit) & 1).astype(jnp.int8)
        flags[bit * width : (bit + 1) * width, :] = flag.astype(F8)
    at = 0
    for bits_ref, count_ref in zip(pairs[::2], pairs[1::2]):
        rows = bits_ref.shape[0]
        common = jnp.dot(bits_ref[...], flags[...], preferred_element_type=jnp.float32)
        union = (count + count_ref[:, 0:1]) - common
        kern[at : at + rows, :] = (common / union).astype(jnp.bfloat16)
        at += rows
    mid = at // 2
    own = jnp.dot(own_ref[...], kern[...], preferred_element_type=jnp.float32)
    out_ref[0] = own.T.astype(jnp.bfloat16)
    sib = jnp.dot(sib_ref[:, mid:], kern[:mid, :], preferred_element_type=jnp.float32)
    sib += jnp.dot(sib_ref[:, :mid], kern[mid:, :], preferred_element_type=jnp.float32)
    out_ref[1] = sib.T.astype(jnp.bfloat16)


def block(words, own, sib, pairs):
    rows, width = words.shape
    cols = own.shape[0]
    hits = own.shape[1]
    flat = [x for pair in pairs for x in pair]
    return pl.pallas_call(
        block_kernel,
        in_specs=[VMEM] * (3 + len(flat)),
        out_specs=VMEM,
        out_shape=jax.ShapeDtypeStruct((2, rows, cols), jnp.bfloat16),
        scratch_shapes=[
            pltpu.VMEM((BITS * width, rows), F8),
            pltpu.VMEM((hits, rows), jnp.bfloat16),
        ],
        compiler_params=pltpu.CompilerParams(vmem_limit_bytes=32 * 2**20),
        cost_estimate=pl.CostEstimate(
            flops=2 * hits * rows * (BITS * width // 2 + 2 * cols),
            bytes_accessed=rows * cols * 4,
            transcendentals=0,
        ),
        name="block",
    )(words, own, sib, *flat)


def gather_kernel(place_ref, *refs):
    out_ref = refs[-1]
    count = (len(refs) - 1) // 2
    for k in range(count):
        own_ref, sib_ref = refs[2 * k], refs[2 * k + 1]
        rows, cols = sib_ref.shape
        col = pl.ds(pl.multiple_of(place_ref[k + 1] * cols, cols), cols)
        side = place_ref[0]
        out_ref[pl.ds(pl.multiple_of(side * rows, rows), rows), col] = own_ref[0]
        out_ref[pl.ds(pl.multiple_of((1 - side) * rows, rows), rows), col] = sib_ref[...]


def small(fingerprints, pick_list, inverse_root):
    hit_rows, width = fingerprints.shape
    devices = lax.axis_size("hit")
    me = lax.axis_index("hit")
    side = lax.axis_index("lm")
    half = hit_rows // 2
    weight = inverse_root[:, 0, :]
    cols = weight.shape[1]
    swap = [(0, 1), (1, 0)]

    def across(x, k):
        return lax.ppermute(x, "hit", [(i, i ^ k) for i in range(devices)])

    def over(x):
        return lax.ppermute(x, "lm", swap)

    other_picks = over(pick_list)
    packed = fingerprints.astype(jnp.uint16)
    mine = lax.dynamic_slice_in_dim(packed, side * half, half)
    theirs = lax.dynamic_slice_in_dim(packed, (1 - side) * half, half)
    order = list(range(devices - 1, 0, -1))
    own_words = {0: mine}
    for k in order:
        own_words[k] = across(mine, k)
    sib_words = {0: theirs}
    for k in order:
        sib_words[k] = over(own_words[k])

    both = jnp.stack([pick_list, other_picks])
    picks = jnp.where(side == 0, both, both[::-1]).reshape(1, -1)
    slots = jnp.arange(devices)
    tops = (slots ^ me) * hit_rows
    base = jnp.concatenate([tops + side * half, tops + (1 - side) * half]).astype(jnp.int32)
    own_sums = spread(base, picks, weight, half)
    sib_sums = over(own_sums)

    own_pairs = dict()
    sib_pairs = dict()
    own_pairs[0], sib_pairs[0] = unpack([mine, theirs])
    near = [k for k in order if k < devices // 2]
    far = [k for k in order if k >= devices // 2]
    for group, words, pairs in (
        (near, own_words, own_pairs),
        (near, sib_words, sib_pairs),
        (far, own_words, own_pairs),
        (far, sib_words, sib_pairs),
    ):
        pairs.update(zip(group, unpack([words[k] for k in group])))
    pairs = [own_pairs[k] for k in range(devices)] + [sib_pairs[k] for k in range(devices)]

    pieces = []
    for k in order + [0]:
        made = block(own_words[k], own_sums, sib_sums, pairs)
        got = made if k == 0 else across(made, k)
        pieces.append((k, got, over(got[1])))

    place = jnp.stack([side] + [k ^ me for k, _, _ in pieces]).astype(jnp.int32)
    flat = [x for _, got, sib in pieces for x in (got, sib)]
    return pl.pallas_call(
        gather_kernel,
        in_specs=[SMEM] + [VMEM] * len(flat),
        out_specs=VMEM,
        out_shape=jax.ShapeDtypeStruct((hit_rows, devices * cols), jnp.bfloat16),
        compiler_params=pltpu.CompilerParams(vmem_limit_bytes=24 * 2**20),
        name="place",
    )(place, *flat)


def large(fingerprints, pick_list, inverse_root):
    hit_rows, width = fingerprints.shape
    devices = lax.axis_size("hit")
    side = lax.axis_index("lm")
    half = hit_rows // 2
    weight = inverse_root[:, 0, :]
    cols = weight.shape[1]
    picks = lax.all_gather(pick_list, "lm", tiled=True)
    words = lax.all_gather(fingerprints, "hit", tiled=True)
    hits = words.shape[0]
    blocks = words.reshape(devices, hit_rows, width)

    def spread_block(index):
        hot = (index * hit_rows + jnp.arange(hit_rows))[:, None] == picks[None, :]
        made = jnp.dot(hot.astype(jnp.bfloat16), weight, preferred_element_type=jnp.float32)
        return made.astype(jnp.bfloat16)

    def flag_block(block_words):
        flags = [((block_words >> bit) & 1).astype(F8) for bit in range(BITS)]
        return jnp.concatenate(flags, axis=1)

    sums = lax.map(spread_block, jnp.arange(devices)).reshape(hits, cols)
    sums = lax.all_gather(sums, "lm", axis=1, tiled=True)
    bits = lax.map(flag_block, blocks).reshape(hits, BITS * width)
    count = jnp.sum(lax.population_count(words), axis=1).astype(jnp.float32)

    def one(index):
        start = index * hit_rows + side * half
        rows = lax.dynamic_slice_in_dim(bits, start, half)
        common = lax.dot_general(
            rows, bits, (((1,), (1,)), ((), ())), preferred_element_type=jnp.float32
        )
        union = lax.dynamic_slice_in_dim(count, start, half)[:, None] + count[None, :] - common
        kernel = (common / union).astype(jnp.bfloat16)
        return jnp.dot(kernel, sums, preferred_element_type=jnp.float32).astype(jnp.bfloat16)

    made = lax.map(one, jnp.arange(devices))
    got = lax.all_to_all(made, "hit", 0, 0, tiled=True)
    got = got.reshape(devices, half, 2, cols).transpose(2, 1, 0, 3)
    got = got.reshape(2, 1, half, devices * cols)
    return lax.all_to_all(got, "lm", 0, 1, tiled=True).reshape(hit_rows, devices * cols)


def local(fingerprints, pick_list, inverse_root):
    if lax.axis_size("hit") > 8:
        return large(fingerprints, pick_list, inverse_root)
    return small(fingerprints, pick_list, inverse_root)


def solution(mesh):
    placed = (P(("lib", "hit"), None), P(("lib", "lm")), P("lib", "lm", "hit"))
    return jax.shard_map(
        local, mesh=mesh, in_specs=placed, out_specs=P(("lib", "hit"), "lm"), check_vma=False
    )
```

time: 395 us -> 119 us (0.30)
  waiting for transfers between devices: 307 us -> 24.6 us
  Pallas kernels: 0 us -> 60.4 us
  local copies, waits for them, and re-layouts: 36.2 us -> 4.16 us
  starting transfers between devices: 0.09 us -> 28 us
  matrix products: 20.7 us -> 0 us
  between operations: 13.1 us -> 0.21 us
  other arithmetic: 10.7 us -> 1.53 us
  blocking collectives: 6.63 us -> 0 us
    all_gather x1 -> x0, waiting for transfers between devices: 220 us -> none  [local(): lax.all_gather(halves, 'hit', axis=1, tiled=True)]
    pmax x1 -> x0, waiting for transfers between devices: 71.4 us -> none  [local(): landmark_words = lax.pmax(picked, 'hit')]
    pallas_call x0 -> x15, Pallas kernels: none -> 60.4 us  [the longest x8 43.9 us: block(): pl.pallas_call(block_kernel, in_specs=[VMEM] * (3 + len(flat)), out_specs...]
    ppermute x0 -> x31, starting transfers between devices: none -> 28 us  [the longest x14 24.4 us: across(): return lax.ppermute(x, 'hit', [(i, i ^ k) for i in range(devices)])]
    ppermute x0 -> x31, waiting for transfers between devices: none -> 24.6 us  [the longest x14 22.2 us: across(): return lax.ppermute(x, 'hit', [(i, i ^ k) for i in range(devices)])]
    dot_general x2 -> x0, matrix products: 20.7 us -> none  [the longest x1 14.7 us: local(): jnp.dot(kernel, lax.all_gather(halves, 'hit', axis=1, tiled=True), prefer...]
    reduce_scatter x1 -> x0, waiting for transfers between devices: 15.1 us -> none  [local(): lax.psum_scatter(partial_sum, 'lm', scatter_dimension=1, tiled=True)]
    reshape x1 -> x0, local copies, waits for them, and re-layouts: 11.7 us -> none  [local(): partial_sum = partial_sum.reshape(hit_rows, hit_devices, 2, block_cols)]
  transfers between devices with their start and end apart: 3 -> 31, of which waited for: 3 -> 11; matrix products, arithmetic and copies ran while one was open for 3% -> 2% of each run, Pallas kernels for 0% -> 36%
where the time goes in v1:
time: 119 us
  Pallas kernels  60.4 us (51%)
  starting transfers between devices  28 us (24%)
  waiting for transfers between devices  24.6 us (21%)
  local copies, waits for them, and re-layouts  4.16 us (3%)
  other arithmetic  1.53 us (1%)
    pallas_call x8, Pallas kernels, block(): pl.pallas_call(block_kernel, in_specs=[VMEM] * (3 + len(flat)), out_specs...  43.9 us
    ppermute x14, starting transfers between devices, across(): return lax.ppermute(x, 'hit', [(i, i ^ k) for i in range(devices)])  24.4 us
    ppermute x14, waiting for transfers between devices, across(): return lax.ppermute(x, 'hit', [(i, i ^ k) for i in range(devices)])  22.2 us
    pallas_call x1, Pallas kernels, spread(): pl.pallas_call(functools.partial(spread_kernel, sub=sub, chunk=chunk), gr...  10.5 us
    pallas_call x5, Pallas kernels, unpack(): pl.pallas_call(unpack_kernel, in_specs=[VMEM] * len(blocks), out_specs=[V...  3.88 us
    ppermute x17, starting transfers between devices, over(): return lax.ppermute(x, 'lm', swap)  3.61 us
  transfers between devices with their start and end apart: 31, of which 11 were waited for; matrix products, arithmetic and copies ran while one was open for 2% of the time, Pallas kernels for 36%

profile of v1, /device:TPU:0, one launch (start us, length us, event | category | flops | bytes accessed | tf_op | source)
XLA Modules:
  0.0 118.9 jit_solution(6793378026335499533)
XLA Ops:
  0.0 0.5 collective-permute-start.1
  0.5 0.1 pad_add_fusion.1.base_ref
  0.5 1.0 collective-permute-done.1
  1.5 0.7 pad_add_fusion
  2.2 0.4 rev.3
  2.6 0.7 select_bitcast_fusion
  3.4 0.0 copy-start
  3.4 1.6 %copy-done = bf16[4096,1,256]{2,0,1:T(8,128)(2,1)S(1)} copy-done((bf16[4096,1,256]{2,0,1:T(8,128)(2,1)S(1)}, bf16[4096,1,256]{2,0,1:T(8,128)(2,1)}, u32[]{:S(2)}) %copy-start) | copy-done | bytes 2097176
  5.0 10.5 %spread.1.own_ref = bf16[256,4096]{1,0:T(8,128)(2,1)S(1)} custom-call(s32[16]{0:T(128)S(1)} %pad_add_fusion.1.base_ref, s32[1,4096]{1,0:T(1,128)S(1)} %bitcast.32, bf16[4096,256]{1,0:T(8,128)(2,1)S(1)} %bitcast.33), custom_call_target="tpu_custom_call" | custom-call | flops 8589934592 | bytes 4194304 | tf_op jit(solution)/shard_map/spread/pallas_call | solution.py:66
  15.5 0.4 collective-permute-start.2
  15.9 3.8 %collective-permute-start.8 = (u16[256,128]{1,0:T(8,128)(2,1)S(1)}, u16[256,128]{1,0:T(8,128)(2,1)S(1)}, u32[]{:S(2)}, u32[]{:S(2)}) collective-permute-start(u16[256,128]{1,0:T(8,128)(2,1)S(1)} %get-tuple-element.70.refs_0_.words_ref), channel_id=1, source_target_pairs={{0,8},{2,10},{4,12},{6,14},{8,0},{10,2},{12,4},{14,6},{1,9},{3,11}... | collective-permute-start | bytes 196616 | tf_op jit(solution)/shard_map/ppermute | solution.py:157
  19.8 1.3 %collective-permute-start.7 = (u16[256,128]{1,0:T(8,128)(2,1)S(1)}, u16[256,128]{1,0:T(8,128)(2,1)S(1)}, u32[]{:S(2)}, u32[]{:S(2)}) collective-permute-start(u16[256,128]{1,0:T(8,128)(2,1)S(1)} %get-tuple-element.70.refs_0_.words_ref), channel_id=1, source_target_pairs={{0,10},{2,8},{4,14},{6,12},{8,2},{10,0},{12,6},{14,4},{1,11},{3,9}... | collective-permute-start | bytes 196616 | tf_op jit(solution)/shard_map/ppermute | solution.py:157
  21.1 3.6 %collective-permute-start.6 = (u16[256,128]{1,0:T(8,128)(2,1)S(1)}, u16[256,128]{1,0:T(8,128)(2,1)S(1)}, u32[]{:S(2)}, u32[]{:S(2)}) collective-permute-start(u16[256,128]{1,0:T(8,128)(2,1)S(1)} %get-tuple-element.70.refs_0_.words_ref), channel_id=1, source_target_pairs={{0,12},{2,14},{4,8},{6,10},{8,4},{10,6},{12,0},{14,2},{1,13},{3,15... | collective-permute-start | bytes 196616 | tf_op jit(solution)/shard_map/ppermute | solution.py:157
  24.7 0.5 collective-permute-start.5
  25.2 0.0 collective-permute-done.8.refs_3_.words_ref
  25.2 0.8 collective-permute-start.4
  26.0 3.4 %collective-permute-done.7.refs_2_.words_ref = u16[256,128]{1,0:T(8,128)(2,1)S(1)} collective-permute-done((u16[256,128]{1,0:T(8,128)(2,1)S(1)}, u16[256,128]{1,0:T(8,128)(2,1)S(1)}, u32[]{:S(2)}, u32[]{:S(2)}) %collective-permute-start.7) | collective-permute-done | bytes 65568 | tf_op jit(solution)/shard_map/ppermute | solution.py:157
  29.3 0.4 collective-permute-start.3
  29.7 2.8 %collective-permute-start = (u16[256,128]{1,0:T(8,128)(2,1)S(1)}, u16[256,128]{1,0:T(8,128)(2,1)S(1)}, u32[]{:S(2)}, u32[]{:S(2)}) collective-permute-start(u16[256,128]{1,0:T(8,128)(2,1)S(1)} %get-tuple-element.70.refs_0_.words_ref), channel_id=1, source_target_pairs={{0,14},{2,12},{4,10},{6,8},{8,6},{10,4},{12,2},{14,0},{1,15},{3,13... | collective-permute-start | bytes 196616 | tf_op jit(solution)/shard_map/ppermute | solution.py:157
  32.5 0.0 collective-permute-done.5.refs_2_.words_ref
  32.5 0.5 collective-permute-start.10
  33.0 1.5 %collective-permute-done.3.refs_0_.words_ref = u16[256,128]{1,0:T(8,128)(2,1)S(1)} collective-permute-done((u16[256,128]{1,0:T(8,128)(2,1)S(1)}, u16[256,128]{1,0:T(8,128)(2,1)S(1)}, u32[]{:S(2)}, u32[]{:S(2)}) %collective-permute-start.3) | collective-permute-done | bytes 65568 | tf_op jit(solution)/shard_map/ppermute | solution.py:157
  34.5 2.3 %collective-permute-done.refs_0_.words_ref = u16[256,128]{1,0:T(8,128)(2,1)S(1)} collective-permute-done((u16[256,128]{1,0:T(8,128)(2,1)S(1)}, u16[256,128]{1,0:T(8,128)(2,1)S(1)}, u32[]{:S(2)}, u32[]{:S(2)}) %collective-permute-start) | collective-permute-done | bytes 65568 | tf_op jit(solution)/shard_map/ppermute | solution.py:157
  36.8 0.5 collective-permute-start.14
  37.3 0.1 collective-permute-start.13
  37.3 0.4 collective-permute-start.12
  37.8 0.5 unpack.5
  38.3 0.7 unpack.6
  39.0 1.0 unpack.7
  40.0 0.7 unpack.8
  40.7 1.0 unpack.9
  41.7 5.4 %block.15.refs_14_ = bf16[2,256,256]{2,1,0:T(8,128)(2,1)S(1)} custom-call(u16[256,128]{1,0:T(8,128)(2,1)S(1)} %get-tuple-element.70.refs_0_.words_ref, bf16[256,4096]{1,0:T(8,128)(2,1)S(1)} %spread.1.own_ref, bf16[256,4096]{1,0:T(8,128)(2,1)} %collective-permute-done.2.sib_ref, f8e4m3fn[256,2048]{1,0:T(32,128)(4,1)S(1)} %get-tuple-element.37.refs_0_, ...), custom_call_target="tpu_custom_call" | custom-call | flops 3221225472 | bytes 262144 | tf_op jit(solution)/shard_map/block/pallas_call | solution.py:115
  47.2 0.1 collective-permute-start.30
  47.3 5.4 %block.8 = bf16[2,256,256]{2,1,0:T(8,128)(2,1)S(1)} custom-call(u16[256,128]{1,0:T(8,128)(2,1)S(1)} %collective-permute-done.refs_0_.words_ref, bf16[256,4096]{1,0:T(8,128)(2,1)S(1)} %spread.1.own_ref, bf16[256,4096]{1,0:T(8,128)(2,1)} %collective-permute-done.2.sib_ref, f8e4m3fn[256,2048]{1,0:T(32,128)(4,1)S(1)} %get-tuple-element.37.refs_0_, ...), custom_call_target="tpu_custom_call" | custom-call | flops 3221225472 | bytes 262144 | tf_op jit(solution)/shard_map/block/pallas_call | solution.py:115
  52.7 2.8 %collective-permute-start.16 = (bf16[2,256,256]{2,1,0:T(8,128)(2,1)S(1)}, bf16[2,256,256]{2,1,0:T(8,128)(2,1)S(1)}, u32[]{:S(2)}, u32[]{:S(2)}) collective-permute-start(bf16[2,256,256]{2,1,0:T(8,128)(2,1)S(1)} %block.8), channel_id=1, source_target_pairs={{0,14},{2,12},{4,10},{6,8},{8,6},{10,4},{12,2},{14,0},{1,15},{3,13... | collective-permute-start | bytes 786440 | tf_op jit(solution)/shard_map/ppermute | solution.py:157
  55.5 5.6 %block.9 = bf16[2,256,256]{2,1,0:T(8,128)(2,1)S(1)} custom-call(u16[256,128]{1,0:T(8,128)(2,1)S(1)} %collective-permute-done.6.refs_1_.words_ref, bf16[256,4096]{1,0:T(8,128)(2,1)S(1)} %spread.1.own_ref, bf16[256,4096]{1,0:T(8,128)(2,1)} %collective-permute-done.2.sib_ref, f8e4m3fn[256,2048]{1,0:T(32,128)(4,1)S(1)} %get-tuple-element.37.refs_0_, ...), custom_call_target="tpu_custom_call" | custom-call | flops 3221225472 | bytes 262144 | tf_op jit(solution)/shard_map/block/pallas_call | solution.py:115
  61.1 1.7 %collective-permute-start.18 = (bf16[2,256,256]{2,1,0:T(8,128)(2,1)S(1)}, bf16[2,256,256]{2,1,0:T(8,128)(2,1)S(1)}, u32[]{:S(2)}, u32[]{:S(2)}) collective-permute-start(bf16[2,256,256]{2,1,0:T(8,128)(2,1)S(1)} %block.9), channel_id=1, source_target_pairs={{0,12},{2,14},{4,8},{6,10},{8,4},{10,6},{12,0},{14,2},{1,13},{3,15... | collective-permute-start | bytes 786440 | tf_op jit(solution)/shard_map/ppermute | solution.py:157
  62.8 5.4 %block.10 = bf16[2,256,256]{2,1,0:T(8,128)(2,1)S(1)} custom-call(u16[256,128]{1,0:T(8,128)(2,1)S(1)} %collective-permute-done.7.refs_2_.words_ref, bf16[256,4096]{1,0:T(8,128)(2,1)S(1)} %spread.1.own_ref, bf16[256,4096]{1,0:T(8,128)(2,1)} %collective-permute-done.2.sib_ref, f8e4m3fn[256,2048]{1,0:T(32,128)(4,1)S(1)} %get-tuple-element.37.refs_0_, ...), custom_call_target="tpu_custom_call" | custom-call | flops 3221225472 | bytes 262144 | tf_op jit(solution)/shard_map/block/pallas_call | solution.py:115
  68.2 0.3 collective-permute-start.20
  68.5 5.4 %block.11 = bf16[2,256,256]{2,1,0:T(8,128)(2,1)S(1)} custom-call(u16[256,128]{1,0:T(8,128)(2,1)S(1)} %collective-permute-done.8.refs_3_.words_ref, bf16[256,4096]{1,0:T(8,128)(2,1)S(1)} %spread.1.own_ref, bf16[256,4096]{1,0:T(8,128)(2,1)} %collective-permute-done.2.sib_ref, f8e4m3fn[256,2048]{1,0:T(32,128)(4,1)S(1)} %get-tuple-element.37.refs_0_, ...), custom_call_target="tpu_custom_call" | custom-call | flops 3221225472 | bytes 262144 | tf_op jit(solution)/shard_map/block/pallas_call | solution.py:115
  73.9 3.1 %collective-permute-start.22 = (bf16[2,256,256]{2,1,0:T(8,128)(2,1)S(1)}, bf16[2,256,256]{2,1,0:T(8,128)(2,1)S(1)}, u32[]{:S(2)}, u32[]{:S(2)}) collective-permute-start(bf16[2,256,256]{2,1,0:T(8,128)(2,1)S(1)} %block.11), channel_id=1, source_target_pairs={{0,8},{2,10},{4,12},{6,14},{8,0},{10,2},{12,4},{14,6},{1,9},{3,11}... | collective-permute-start | bytes 786440 | tf_op jit(solution)/shard_map/ppermute | solution.py:157
  77.1 5.7 %block.14 = bf16[2,256,256]{2,1,0:T(8,128)(2,1)S(1)} custom-call(u16[256,128]{1,0:T(8,128)(2,1)S(1)} %collective-permute-done.5.refs_2_.words_ref, bf16[256,4096]{1,0:T(8,128)(2,1)S(1)} %spread.1.own_ref, bf16[256,4096]{1,0:T(8,128)(2,1)} %collective-permute-done.2.sib_ref, f8e4m3fn[256,2048]{1,0:T(32,128)(4,1)S(1)} %get-tuple-element.37.refs_0_, ...), custom_call_target="tpu_custom_call" | custom-call | flops 3221225472 | bytes 262144 | tf_op jit(solution)/shard_map/block/pallas_call | solution.py:115
  82.7 5.5 %block.13 = bf16[2,256,256]{2,1,0:T(8,128)(2,1)S(1)} custom-call(u16[256,128]{1,0:T(8,128)(2,1)S(1)} %collective-permute-done.4.refs_1_.words_ref, bf16[256,4096]{1,0:T(8,128)(2,1)S(1)} %spread.1.own_ref, bf16[256,4096]{1,0:T(8,128)(2,1)} %collective-permute-done.2.sib_ref, f8e4m3fn[256,2048]{1,0:T(32,128)(4,1)S(1)} %get-tuple-element.37.refs_0_, ...), custom_call_target="tpu_custom_call" | custom-call | flops 3221225472 | bytes 262144 | tf_op jit(solution)/shard_map/block/pallas_call | solution.py:115
  88.2 5.5 %block.12 = bf16[2,256,256]{2,1,0:T(8,128)(2,1)S(1)} custom-call(u16[256,128]{1,0:T(8,128)(2,1)S(1)} %collective-permute-done.3.refs_0_.words_ref, bf16[256,4096]{1,0:T(8,128)(2,1)S(1)} %spread.1.own_ref, bf16[256,4096]{1,0:T(8,128)(2,1)} %collective-permute-done.2.sib_ref, f8e4m3fn[256,2048]{1,0:T(32,128)(4,1)S(1)} %get-tuple-element.37.refs_0_, ...), custom_call_target="tpu_custom_call" | custom-call | flops 3221225472 | bytes 262144 | tf_op jit(solution)/shard_map/block/pallas_call | solution.py:115
  93.7 1.1 collective-permute-start.24
  94.9 1.5 %collective-permute-start.26 = (bf16[2,256,256]{2,1,0:T(8,128)(2,1)S(1)}, bf16[2,256,256]{2,1,0:T(8,128)(2,1)S(1)}, u32[]{:S(2)}, u32[]{:S(2)}) collective-permute-start(bf16[2,256,256]{2,1,0:T(8,128)(2,1)S(1)} %block.13), channel_id=1, source_target_pairs={{0,4},{2,6},{4,0},{6,2},{8,12},{10,14},{12,8},{14,10},{1,5},{3,7},... | collective-permute-start | bytes 786440 | tf_op jit(solution)/shard_map/ppermute | solution.py:157
  96.4 0.8 collective-permute-done.20.refs_4_
  97.2 0.7 collective-permute-start.28
  97.9 3.8 %collective-permute-done.22.refs_6_ = bf16[2,256,256]{2,1,0:T(8,128)(2,1)S(1)} collective-permute-done((bf16[2,256,256]{2,1,0:T(8,128)(2,1)S(1)}, bf16[2,256,256]{2,1,0:T(8,128)(2,1)S(1)}, u32[]{:S(2)}, u32[]{:S(2)}) %collective-permute-start.22) | collective-permute-done | bytes 262176 | tf_op jit(solution)/shard_map/ppermute | solution.py:157
  101.7 6.4 %collective-permute-done.24.refs_8_ = bf16[2,256,256]{2,1,0:T(8,128)(2,1)S(1)} collective-permute-done((bf16[2,256,256]{2,1,0:T(8,128)(2,1)S(1)}, bf16[2,256,256]{2,1,0:T(8,128)(2,1)S(1)}, u32[]{:S(2)}, u32[]{:S(2)}) %collective-permute-start.24) | collective-permute-done | bytes 262176 | tf_op jit(solution)/shard_map/ppermute | solution.py:157
  108.1 0.7 slice_bitcast_fusion.3
  108.7 4.1 %collective-permute-done.26.refs_10_ = bf16[2,256,256]{2,1,0:T(8,128)(2,1)S(1)} collective-permute-done((bf16[2,256,256]{2,1,0:T(8,128)(2,1)S(1)}, bf16[2,256,256]{2,1,0:T(8,128)(2,1)S(1)}, u32[]{:S(2)}, u32[]{:S(2)}) %collective-permute-start.26) | collective-permute-done | bytes 262176 | tf_op jit(solution)/shard_map/ppermute | solution.py:157
  112.8 0.0 collective-permute-start.21
  112.9 0.6 slice_bitcast_fusion.2
  113.5 0.5 collective-permute-start.23
  114.0 0.7 slice_bitcast_fusion.1
  114.7 0.0 collective-permute-start.25
  114.7 0.5 collective-permute-start.27
  115.2 0.1 collective-permute-start.29
  115.3 0.1 stack.48.place_ref
  115.4 0.9 collective-permute-done.25.refs_9_
  116.2 0.2 collective-permute-done.27.refs_11_
  116.4 0.3 collective-permute-done.29.refs_13_
  116.7 2.1 %place.1 = bf16[512,2048]{1,0:T(8,128)(2,1)} custom-call(s32[9]{0:T(128)S(1)} %stack.48.place_ref, bf16[2,256,256]{2,1,0:T(8,128)(2,1)S(1)} %collective-permute-done.16.refs_0_, bf16[256,256]{1,0:T(8,128)(2,1)S(1)} %collective-permute-done.17.refs_1_, bf16[2,256,256]{2,1,0:T(8,128)(2,1)S(1)} %collective-permute-done.18.refs_2_, ...), custom_call_target="tpu_custom_call" | custom-call | tf_op jit(solution)/shard_map/place/pallas_call | solution.py:204
  (34 shorter events, 0.2 us)
Async XLA Ops:
  0.0 1.5 %collective-permute-start.1 = (s32[2048]{0:T(1024)}, s32[2048]{0:T(1024)S(1)}, u32[]{:S(2)}, u32[]{:S(2)}) collective-permute-start(s32[2048]{0:T(1024)} %param.4), channel_id=1, source_target_pairs={{0,1},{1,0},{2,3},{3,2},{4,5},{5,4},{6,7},{7,6},{8,9},{9,8},{10,11... | collective-permute-start | bytes 24584 | tf_op jit(solution)/shard_map/ppermute | solution.py:160
  3.4 1.6 %copy-start = (bf16[4096,1,256]{2,0,1:T(8,128)(2,1)S(1)}, bf16[4096,1,256]{2,0,1:T(8,128)(2,1)}, u32[]{:S(2)}) copy-start(bf16[4096,1,256]{2,0,1:T(8,128)(2,1)} %param.5) | copy-start | bytes 6291460
  5.0 10.9 %copy-start.1 = (s32[512,128]{1,0:T(8,128)S(1)}, s32[512,128]{1,0:T(8,128)}, u32[]{:S(2)}) copy-start(s32[512,128]{1,0:T(8,128)} %param.3) | copy-start | bytes 786436
  15.5 26.2 %collective-permute-start.2 = (bf16[256,4096]{1,0:T(8,128)(2,1)S(1)}, bf16[256,4096]{1,0:T(8,128)(2,1)}, u32[]{:S(2)}, u32[]{:S(2)}) collective-permute-start(bf16[256,4096]{1,0:T(8,128)(2,1)S(1)} %spread.1.own_ref), channel_id=1, source_target_pairs={{0,1},{1,0},{2,3},{3,2},{4,5},{5,4},{6,7},{7,6},{8,9},{9,8},{10,11... | collective-permute-start | bytes 6291464 | tf_op jit(solution)/shard_map/ppermute | solution.py:160
  15.9 9.2 %collective-permute-start.8 = (u16[256,128]{1,0:T(8,128)(2,1)S(1)}, u16[256,128]{1,0:T(8,128)(2,1)S(1)}, u32[]{:S(2)}, u32[]{:S(2)}) collective-permute-start(u16[256,128]{1,0:T(8,128)(2,1)S(1)} %get-tuple-element.70.refs_0_.words_ref), channel_id=1, source_target_pairs={{0,8},{2,10},{4,12},{6,14},{8,0},{10,2},{12,4},{14,6},{1,9},{3,11}... | collective-permute-start | bytes 196616 | tf_op jit(solution)/shard_map/ppermute | solution.py:157
  19.8 9.6 %collective-permute-start.7 = (u16[256,128]{1,0:T(8,128)(2,1)S(1)}, u16[256,128]{1,0:T(8,128)(2,1)S(1)}, u32[]{:S(2)}, u32[]{:S(2)}) collective-permute-start(u16[256,128]{1,0:T(8,128)(2,1)S(1)} %get-tuple-element.70.refs_0_.words_ref), channel_id=1, source_target_pairs={{0,10},{2,8},{4,14},{6,12},{8,2},{10,0},{12,6},{14,4},{1,11},{3,9}... | collective-permute-start | bytes 196616 | tf_op jit(solution)/shard_map/ppermute | solution.py:157
  21.1 8.6 %collective-permute-start.6 = (u16[256,128]{1,0:T(8,128)(2,1)S(1)}, u16[256,128]{1,0:T(8,128)(2,1)S(1)}, u32[]{:S(2)}, u32[]{:S(2)}) collective-permute-start(u16[256,128]{1,0:T(8,128)(2,1)S(1)} %get-tuple-element.70.refs_0_.words_ref), channel_id=1, source_target_pairs={{0,12},{2,14},{4,8},{6,10},{8,4},{10,6},{12,0},{14,2},{1,13},{3,15... | collective-permute-start | bytes 196616 | tf_op jit(solution)/shard_map/ppermute | solution.py:157
  24.7 7.8 %collective-permute-start.5 = (u16[256,128]{1,0:T(8,128)(2,1)S(1)}, u16[256,128]{1,0:T(8,128)(2,1)S(1)}, u32[]{:S(2)}, u32[]{:S(2)}) collective-permute-start(u16[256,128]{1,0:T(8,128)(2,1)S(1)} %get-tuple-element.70.refs_0_.words_ref), channel_id=1, source_target_pairs={{0,2},{2,0},{4,6},{6,4},{8,10},{10,8},{12,14},{14,12},{1,3},{3,1},... | collective-permute-start | bytes 196616 | tf_op jit(solution)/shard_map/ppermute | solution.py:157
  25.2 7.3 %collective-permute-start.4 = (u16[256,128]{1,0:T(8,128)(2,1)S(1)}, u16[256,128]{1,0:T(8,128)(2,1)S(1)}, u32[]{:S(2)}, u32[]{:S(2)}) collective-permute-start(u16[256,128]{1,0:T(8,128)(2,1)S(1)} %get-tuple-element.70.refs_0_.words_ref), channel_id=1, source_target_pairs={{0,4},{2,6},{4,0},{6,2},{8,12},{10,14},{12,8},{14,10},{1,5},{3,7},... | collective-permute-start | bytes 196616 | tf_op jit(solution)/shard_map/ppermute | solution.py:157
  29.3 5.2 %collective-permute-start.3 = (u16[256,128]{1,0:T(8,128)(2,1)S(1)}, u16[256,128]{1,0:T(8,128)(2,1)S(1)}, u32[]{:S(2)}, u32[]{:S(2)}) collective-permute-start(u16[256,128]{1,0:T(8,128)(2,1)S(1)} %get-tuple-element.70.refs_0_.words_ref), channel_id=1, source_target_pairs={{0,6},{2,4},{4,2},{6,0},{8,14},{10,12},{12,10},{14,8},{1,7},{3,5},... | collective-permute-start | bytes 196616 | tf_op jit(solution)/shard_map/ppermute | solution.py:157
  29.7 7.0 %collective-permute-start = (u16[256,128]{1,0:T(8,128)(2,1)S(1)}, u16[256,128]{1,0:T(8,128)(2,1)S(1)}, u32[]{:S(2)}, u32[]{:S(2)}) collective-permute-start(u16[256,128]{1,0:T(8,128)(2,1)S(1)} %get-tuple-element.70.refs_0_.words_ref), channel_id=1, source_target_pairs={{0,14},{2,12},{4,10},{6,8},{8,6},{10,4},{12,2},{14,0},{1,15},{3,13... | collective-permute-start | bytes 196616 | tf_op jit(solution)/shard_map/ppermute | solution.py:157
  32.5 4.3 %collective-permute-start.11 = (u16[256,128]{1,0:T(8,128)(2,1)S(1)}, u16[256,128]{1,0:T(8,128)(2,1)S(1)}, u32[]{:S(2)}, u32[]{:S(2)}) collective-permute-start(u16[256,128]{1,0:T(8,128)(2,1)S(1)} %collective-permute-done.5.refs_2_.words_ref), channel_id=1, source_target_pairs={{0,1},{1,0},{2,3},{3,2},{4,5},{5,4},{6,7},{7,6},{8,9},{9,8},{10,11... | collective-permute-start | bytes 196616 | tf_op jit(solution)/shard_map/ppermute | solution.py:160
  32.5 4.8 %collective-permute-start.10 = (u16[256,128]{1,0:T(8,128)(2,1)S(1)}, u16[256,128]{1,0:T(8,128)(2,1)S(1)}, u32[]{:S(2)}, u32[]{:S(2)}) collective-permute-start(u16[256,128]{1,0:T(8,128)(2,1)S(1)} %collective-permute-done.4.refs_1_.words_ref), channel_id=1, source_target_pairs={{0,1},{1,0},{2,3},{3,2},{4,5},{5,4},{6,7},{7,6},{8,9},{9,8},{10,11... | collective-permute-start | bytes 196616 | tf_op jit(solution)/shard_map/ppermute | solution.py:160
  34.5 2.9 %collective-permute-start.9 = (u16[256,128]{1,0:T(8,128)(2,1)S(1)}, u16[256,128]{1,0:T(8,128)(2,1)S(1)}, u32[]{:S(2)}, u32[]{:S(2)}) collective-permute-start(u16[256,128]{1,0:T(8,128)(2,1)S(1)} %collective-permute-done.3.refs_0_.words_ref), channel_id=1, source_target_pairs={{0,1},{1,0},{2,3},{3,2},{4,5},{5,4},{6,7},{7,6},{8,9},{9,8},{10,11... | collective-permute-start | bytes 196616 | tf_op jit(solution)/shard_map/ppermute | solution.py:160
  36.8 4.0 %collective-permute-start.15 = (u16[256,128]{1,0:T(8,128)(2,1)S(1)}, u16[256,128]{1,0:T(8,128)(2,1)S(1)}, u32[]{:S(2)}, u32[]{:S(2)}) collective-permute-start(u16[256,128]{1,0:T(8,128)(2,1)S(1)} %collective-permute-done.8.refs_3_.words_ref), channel_id=1, source_target_pairs={{0,1},{1,0},{2,3},{3,2},{4,5},{5,4},{6,7},{7,6},{8,9},{9,8},{10,11... | collective-permute-start | bytes 196616 | tf_op jit(solution)/shard_map/ppermute | solution.py:160
  36.8 4.0 %collective-permute-start.14 = (u16[256,128]{1,0:T(8,128)(2,1)S(1)}, u16[256,128]{1,0:T(8,128)(2,1)S(1)}, u32[]{:S(2)}, u32[]{:S(2)}) collective-permute-start(u16[256,128]{1,0:T(8,128)(2,1)S(1)} %collective-permute-done.7.refs_2_.words_ref), channel_id=1, source_target_pairs={{0,1},{1,0},{2,3},{3,2},{4,5},{5,4},{6,7},{7,6},{8,9},{9,8},{10,11... | collective-permute-start | bytes 196616 | tf_op jit(solution)/shard_map/ppermute | solution.py:160
  37.3 3.5 %collective-permute-start.13 = (u16[256,128]{1,0:T(8,128)(2,1)S(1)}, u16[256,128]{1,0:T(8,128)(2,1)S(1)}, u32[]{:S(2)}, u32[]{:S(2)}) collective-permute-start(u16[256,128]{1,0:T(8,128)(2,1)S(1)} %collective-permute-done.6.refs_1_.words_ref), channel_id=1, source_target_pairs={{0,1},{1,0},{2,3},{3,2},{4,5},{5,4},{6,7},{7,6},{8,9},{9,8},{10,11... | collective-permute-start | bytes 196616 | tf_op jit(solution)/shard_map/ppermute | solution.py:160
  37.3 3.4 %collective-permute-start.12 = (u16[256,128]{1,0:T(8,128)(2,1)S(1)}, u16[256,128]{1,0:T(8,128)(2,1)S(1)}, u32[]{:S(2)}, u32[]{:S(2)}) collective-permute-start(u16[256,128]{1,0:T(8,128)(2,1)S(1)} %collective-permute-done.refs_0_.words_ref), channel_id=1, source_target_pairs={{0,1},{1,0},{2,3},{3,2},{4,5},{5,4},{6,7},{7,6},{8,9},{9,8},{10,11... | collective-permute-start | bytes 196616 | tf_op jit(solution)/shard_map/ppermute | solution.py:160
  47.2 67.5 %collective-permute-start.30 = (bf16[256,256]{1,0:T(8,128)(2,1)S(1)}, bf16[256,256]{1,0:T(8,128)(2,1)S(1)}, u32[]{:S(2)}, u32[]{:S(2)}) collective-permute-start(bf16[256,256]{1,0:T(8,128)(2,1)S(1)} %slice_bitcast_fusion), channel_id=1, source_target_pairs={{0,1},{1,0},{2,3},{3,2},{4,5},{5,4},{6,7},{7,6},{8,9},{9,8},{10,11... | collective-permute-start | bytes 393224 | tf_op jit(solution)/shard_map/ppermute | solution.py:160
  52.7 41.0 %collective-permute-start.16 = (bf16[2,256,256]{2,1,0:T(8,128)(2,1)S(1)}, bf16[2,256,256]{2,1,0:T(8,128)(2,1)S(1)}, u32[]{:S(2)}, u32[]{:S(2)}) collective-permute-start(bf16[2,256,256]{2,1,0:T(8,128)(2,1)S(1)} %block.8), channel_id=1, source_target_pairs={{0,14},{2,12},{4,10},{6,8},{8,6},{10,4},{12,2},{14,0},{1,15},{3,13... | collective-permute-start | bytes 786440 | tf_op jit(solution)/shard_map/ppermute | solution.py:157
  61.1 33.8 %collective-permute-start.18 = (bf16[2,256,256]{2,1,0:T(8,128)(2,1)S(1)}, bf16[2,256,256]{2,1,0:T(8,128)(2,1)S(1)}, u32[]{:S(2)}, u32[]{:S(2)}) collective-permute-start(bf16[2,256,256]{2,1,0:T(8,128)(2,1)S(1)} %block.9), channel_id=1, source_target_pairs={{0,12},{2,14},{4,8},{6,10},{8,4},{10,6},{12,0},{14,2},{1,13},{3,15... | collective-permute-start | bytes 786440 | tf_op jit(solution)/shard_map/ppermute | solution.py:157
  68.2 29.0 %collective-permute-start.20 = (bf16[2,256,256]{2,1,0:T(8,128)(2,1)S(1)}, bf16[2,256,256]{2,1,0:T(8,128)(2,1)S(1)}, u32[]{:S(2)}, u32[]{:S(2)}) collective-permute-start(bf16[2,256,256]{2,1,0:T(8,128)(2,1)S(1)} %block.10), channel_id=1, source_target_pairs={{0,10},{2,8},{4,14},{6,12},{8,2},{10,0},{12,6},{14,4},{1,11},{3,9}... | collective-permute-start | bytes 786440 | tf_op jit(solution)/shard_map/ppermute | solution.py:157
  73.9 27.7 %collective-permute-start.22 = (bf16[2,256,256]{2,1,0:T(8,128)(2,1)S(1)}, bf16[2,256,256]{2,1,0:T(8,128)(2,1)S(1)}, u32[]{:S(2)}, u32[]{:S(2)}) collective-permute-start(bf16[2,256,256]{2,1,0:T(8,128)(2,1)S(1)} %block.11), channel_id=1, source_target_pairs={{0,8},{2,10},{4,12},{6,14},{8,0},{10,2},{12,4},{14,6},{1,9},{3,11}... | collective-permute-start | bytes 786440 | tf_op jit(solution)/shard_map/ppermute | solution.py:157
  93.7 14.4 %collective-permute-start.24 = (bf16[2,256,256]{2,1,0:T(8,128)(2,1)S(1)}, bf16[2,256,256]{2,1,0:T(8,128)(2,1)S(1)}, u32[]{:S(2)}, u32[]{:S(2)}) collective-permute-start(bf16[2,256,256]{2,1,0:T(8,128)(2,1)S(1)} %block.12), channel_id=1, source_target_pairs={{0,6},{2,4},{4,2},{6,0},{8,14},{10,12},{12,10},{14,8},{1,7},{3,5},... | collective-permute-start | bytes 786440 | tf_op jit(solution)/shard_map/ppermute | solution.py:157
  94.9 18.0 %collective-permute-start.26 = (bf16[2,256,256]{2,1,0:T(8,128)(2,1)S(1)}, bf16[2,256,256]{2,1,0:T(8,128)(2,1)S(1)}, u32[]{:S(2)}, u32[]{:S(2)}) collective-permute-start(bf16[2,256,256]{2,1,0:T(8,128)(2,1)S(1)} %block.13), channel_id=1, source_target_pairs={{0,4},{2,6},{4,0},{6,2},{8,12},{10,14},{12,8},{14,10},{1,5},{3,7},... | collective-permute-start | bytes 786440 | tf_op jit(solution)/shard_map/ppermute | solution.py:157
  97.2 16.3 %collective-permute-start.28 = (bf16[2,256,256]{2,1,0:T(8,128)(2,1)S(1)}, bf16[2,256,256]{2,1,0:T(8,128)(2,1)S(1)}, u32[]{:S(2)}, u32[]{:S(2)}) collective-permute-start(bf16[2,256,256]{2,1,0:T(8,128)(2,1)S(1)} %block.14), channel_id=1, source_target_pairs={{0,2},{2,0},{4,6},{6,4},{8,10},{10,8},{12,14},{14,12},{1,3},{3,1},... | collective-permute-start | bytes 786440 | tf_op jit(solution)/shard_map/ppermute | solution.py:157
  101.7 13.0 %collective-permute-start.17 = (bf16[256,256]{1,0:T(8,128)(2,1)S(1)}, bf16[256,256]{1,0:T(8,128)(2,1)S(1)}, u32[]{:S(2)}, u32[]{:S(2)}) collective-permute-start(bf16[256,256]{1,0:T(8,128)(2,1)S(1)} %slice_bitcast_fusion.7), channel_id=1, source_target_pairs={{0,1},{1,0},{2,3},{3,2},{4,5},{5,4},{6,7},{7,6},{8,9},{9,8},{10,11... | collective-permute-start | bytes 393224 | tf_op jit(solution)/shard_map/ppermute | solution.py:160
  108.1 7.1 %collective-permute-start.19 = (bf16[256,256]{1,0:T(8,128)(2,1)S(1)}, bf16[256,256]{1,0:T(8,128)(2,1)S(1)}, u32[]{:S(2)}, u32[]{:S(2)}) collective-permute-start(bf16[256,256]{1,0:T(8,128)(2,1)S(1)} %slice_bitcast_fusion.6), channel_id=1, source_target_pairs={{0,1},{1,0},{2,3},{3,2},{4,5},{5,4},{6,7},{7,6},{8,9},{9,8},{10,11... | collective-permute-start | bytes 393224 | tf_op jit(solution)/shard_map/ppermute | solution.py:160
  112.8 2.5 %collective-permute-start.21 = (bf16[256,256]{1,0:T(8,128)(2,1)S(1)}, bf16[256,256]{1,0:T(8,128)(2,1)S(1)}, u32[]{:S(2)}, u32[]{:S(2)}) collective-permute-start(bf16[256,256]{1,0:T(8,128)(2,1)S(1)} %slice_bitcast_fusion.5), channel_id=1, source_target_pairs={{0,1},{1,0},{2,3},{3,2},{4,5},{5,4},{6,7},{7,6},{8,9},{9,8},{10,11... | collective-permute-start | bytes 393224 | tf_op jit(solution)/shard_map/ppermute | solution.py:160
  113.5 1.8 %collective-permute-start.23 = (bf16[256,256]{1,0:T(8,128)(2,1)S(1)}, bf16[256,256]{1,0:T(8,128)(2,1)S(1)}, u32[]{:S(2)}, u32[]{:S(2)}) collective-permute-start(bf16[256,256]{1,0:T(8,128)(2,1)S(1)} %slice_bitcast_fusion.4), channel_id=1, source_target_pairs={{0,1},{1,0},{2,3},{3,2},{4,5},{5,4},{6,7},{7,6},{8,9},{9,8},{10,11... | collective-permute-start | bytes 393224 | tf_op jit(solution)/shard_map/ppermute | solution.py:160
  114.7 1.6 %collective-permute-start.25 = (bf16[256,256]{1,0:T(8,128)(2,1)}, bf16[256,256]{1,0:T(8,128)(2,1)S(1)}, u32[]{:S(2)}, u32[]{:S(2)}) collective-permute-start(bf16[256,256]{1,0:T(8,128)(2,1)} %slice_bitcast_fusion.3), channel_id=1, source_target_pairs={{0,1},{1,0},{2,3},{3,2},{4,5},{5,4},{6,7},{7,6},{8,9},{9,8},{10,11... | collective-permute-start | bytes 393224 | tf_op jit(solution)/shard_map/ppermute | solution.py:160
  114.7 1.7 %collective-permute-start.27 = (bf16[256,256]{1,0:T(8,128)(2,1)}, bf16[256,256]{1,0:T(8,128)(2,1)S(1)}, u32[]{:S(2)}, u32[]{:S(2)}) collective-permute-start(bf16[256,256]{1,0:T(8,128)(2,1)} %slice_bitcast_fusion.2), channel_id=1, source_target_pairs={{0,1},{1,0},{2,3},{3,2},{4,5},{5,4},{6,7},{7,6},{8,9},{9,8},{10,11... | collective-permute-start | bytes 393224 | tf_op jit(solution)/shard_map/ppermute | solution.py:160
  115.2 1.6 %collective-permute-start.29 = (bf16[256,256]{1,0:T(8,128)(2,1)}, bf16[256,256]{1,0:T(8,128)(2,1)S(1)}, u32[]{:S(2)}, u32[]{:S(2)}) collective-permute-start(bf16[256,256]{1,0:T(8,128)(2,1)} %slice_bitcast_fusion.1), channel_id=1, source_target_pairs={{0,1},{1,0},{2,3},{3,2},{4,5},{5,4},{6,7},{7,6},{8,9},{9,8},{10,11... | collective-permute-start | bytes 393224 | tf_op jit(solution)/shard_map/ppermute | solution.py:160
